TPU v7x, 32 devices: a whole 2x2x4 slice. The times are simulated.
32 devices in a mesh: grp: 4 (over y, x), dev: 8 (over z, core).
Axes of the slice: x: 2, y: 2, z: 4, core: 2. Of those that a mesh axis runs over, the one named last changes fastest.
Arguments:
- child_weights: float32 [2, 256, 4, 64, 64], P(None, ('grp', 'dev')), may hold values from -0.12 to 0.12
- pivots: int32 [256, 32], P(('grp', 'dev')), may hold values from 0 to 1023, as said below
- ranks: int32 [256], replicated, may hold values from 1 to 32, 2560 in all
- owner_slot: int32 [256], replicated, may hold values from 0 to 255, each once
Outputs:
- skeleton_sums: float32 [2, 32, 256, 64], P(None, None, ('grp', 'dev'))
Inputs may be any that keep to these rules, and one draw needn't show every extreme that they name: `pivots`: each row lists 32 distinct points of one target box, numbered row by row within the box. The ranks sum to 2560; some box has rank 32. A permutation: box a is owned by device floor(owner_slot[a] / 8) of grp+dev, at place owner_slot[a] mod 8.
All inputs are finite; a program needn't handle non-finite values.
Results may differ from a plain program's by a relative error of at most 0.0003.
Values sent between devices are 32-bit elements; how exact they have to be, the bound alone decides.
A program may use at most 64 MiB of HBM per device.

v0:
```python
import math

import jax
import jax.numpy as jnp
from jax import lax
from jax.sharding import PartitionSpec as P

GRID = 2048
Q = 8
RT = 32


TWO_PI = 2.0 * math.pi
speed_waves = 8


def cheb_nodes(degree):
    steps_j = jnp.arange(degree, dtype=jnp.float32)
    return jnp.cos(math.pi * (2.0 * steps_j + 1.0) / (2.0 * degree))


def lagrange_table(nodes_at, points):
    degree = nodes_at.shape[0]
    differ = points[None, :] - nodes_at[:, None]
    diagonal_mask = jnp.eye(degree, dtype=bool)
    factors = jnp.where(diagonal_mask[:, :, None], 1.0, differ[None, :, :])
    numerator = jnp.prod(factors, axis=1)
    node_gaps = nodes_at[:, None] - nodes_at[None, :] + jnp.eye(degree, dtype=nodes_at.dtype)
    return numerator / jnp.prod(node_gaps, axis=1)[:, None]


def child_table(degree):
    chebyshev = cheb_nodes(degree)
    halves = jnp.stack(
        [lagrange_table(chebyshev, child_side - 0.5 + 0.5 * chebyshev) for child_side in (0.0, 1.0)]
    )
    interp_table = jnp.einsum("uaj,vbk->abuvjk", halves, halves)
    return interp_table.reshape(degree * degree, 4 * degree * degree)


def proxy_offsets(degree, grid_cells):
    chebyshev = cheb_nodes(degree)
    source_side = grid_cells // 32
    quarter = source_side / 4.0
    child_half = jnp.arange(2, dtype=jnp.float32) * (source_side / 2.0)
    along = child_half[:, None] + (quarter - 0.5) + quarter * chebyshev[None, :]
    child_x = jnp.broadcast_to(along[:, None, :, None], (2, 2, degree, degree)).reshape(-1)
    child_y = jnp.broadcast_to(along[None, :, None, :], (2, 2, degree, degree)).reshape(-1)
    parent_along = source_side / 2.0 - 0.5 + source_side / 2.0 * chebyshev
    parent_x = jnp.broadcast_to(parent_along[:, None], (degree, degree)).reshape(-1)
    parent_y = jnp.broadcast_to(parent_along[None, :], (degree, degree)).reshape(-1)
    return (child_x, child_y, parent_x, parent_y)


def phase_cycles(head_x, head_y, denominator, corner_x, corner_y, shift_x, shift_y):
    whole_part = (
        jnp.mod(head_x * corner_x + head_y * corner_y, denominator).astype(jnp.float32)
        / denominator
    )
    place_x = head_x.astype(jnp.float32) / denominator
    place_y = head_y.astype(jnp.float32) / denominator
    turn_x = TWO_PI * jnp.mod(speed_waves * head_x, denominator).astype(jnp.float32) / denominator
    turn_y = TWO_PI * jnp.mod(speed_waves * head_y, denominator).astype(jnp.float32) / denominator
    speed_x = (2.0 + jnp.sin(turn_x) * jnp.sin(turn_y)) / 16.0
    speed_y = (2.0 + jnp.cos(turn_x) * jnp.cos(turn_y)) / 16.0
    freq_x = corner_x.astype(jnp.float32) + shift_x
    freq_y = corner_y.astype(jnp.float32) + shift_y
    return (
        whole_part
        + place_x * shift_x
        + place_y * shift_y
        + jnp.sqrt((speed_x * freq_x) ** 2 + (speed_y * freq_y) ** 2)
    )


def target_centres(box_ids, grid_cells):
    target_side = grid_cells // 64
    target_row = grid_cells // 32
    return (
        2 * (box_ids // target_row) * target_side + target_side - 1,
        2 * (box_ids % target_row) * target_side + target_side - 1,
    )


def pivot_points(box_ids, pivot_ids, grid_cells):
    target_side = grid_cells // 64
    target_row = grid_cells // 32
    return (
        box_ids // target_row * target_side + pivot_ids // target_side,
        box_ids % target_row * target_side + pivot_ids % target_side,
    )


def source_box(child_box, box_id, centre_x, centre_y, offsets, interp_table, grid_cells):
    child_x, child_y, parent_x, parent_y = offsets
    corner_x = box_id // (grid_cells // 64) * (grid_cells // 32) - grid_cells // 2
    corner_y = box_id % (grid_cells // 64) * (grid_cells // 32) - grid_cells // 2
    half_row = grid_cells // 64
    inner = child_box.shape[1]
    parents = child_box.shape[2]
    spread = child_box.reshape(2, inner, parents // half_row, 1, half_row, 1)
    spread = jnp.broadcast_to(spread, (2, inner, parents // half_row, 2, half_row, 2)).reshape(
        2, inner, 4 * parents
    )
    phase_now = TWO_PI * phase_cycles(
        centre_x[None, :],
        centre_y[None, :],
        2 * grid_cells,
        corner_x,
        corner_y,
        child_x[:, None],
        child_y[:, None],
    )
    cosine = jnp.cos(phase_now)
    sine_part = jnp.sin(phase_now)
    stacked = jnp.stack(
        [spread[0] * cosine + spread[1] * sine_part, spread[1] * cosine - spread[0] * sine_part]
    )
    interp = jnp.einsum("tc,zca->zta", interp_table, stacked, precision=lax.Precision.HIGHEST)
    phase_back = TWO_PI * phase_cycles(
        centre_x[None, :],
        centre_y[None, :],
        2 * grid_cells,
        corner_x,
        corner_y,
        parent_x[:, None],
        parent_y[:, None],
    )
    cosine_back = jnp.cos(phase_back)
    sine_back = jnp.sin(phase_back)
    return jnp.stack(
        [
            interp[0] * cosine_back - interp[1] * sine_back,
            interp[0] * sine_back + interp[1] * cosine_back,
        ]
    )


def skeleton_rows(point_x, point_y, box_ids, weights, offsets, grid_cells):
    parent_x = offsets[2]
    parent_y = offsets[3]
    corner_x = box_ids // (grid_cells // 64) * (grid_cells // 32) - grid_cells // 2
    corner_y = box_ids % (grid_cells // 64) * (grid_cells // 32) - grid_cells // 2
    phase_now = TWO_PI * phase_cycles(
        point_x[None, None, :],
        point_y[None, None, :],
        grid_cells,
        corner_x[:, None, None],
        corner_y[:, None, None],
        parent_x[None, :, None],
        parent_y[None, :, None],
    )
    cosine = jnp.cos(phase_now)
    sine_part = jnp.sin(phase_now)
    real_sum = jnp.sum(cosine * weights[:, 0] - sine_part * weights[:, 1], axis=1)
    imag_sum = jnp.sum(sine_part * weights[:, 0] + cosine * weights[:, 1], axis=1)
    return jnp.stack([real_sum, imag_sum])


def route(outgoing, per_owner):
    inner = outgoing.shape[2]
    received = lax.all_to_all(outgoing, ("grp", "dev"), split_axis=3, concat_axis=0, tiled=True)
    return received.reshape(received.shape[0], 2, inner, per_owner)


def local(child_weights, pivots, ranks, owner_slot):
    grid_cells = GRID
    group_size = lax.axis_size("grp") * lax.axis_size("dev")
    position = lax.axis_index("grp") * lax.axis_size("dev") + lax.axis_index("dev")
    own_boxes = child_weights.shape[1]
    proxies = Q * Q
    targets_all = ranks.shape[0]
    per_owner = targets_all // group_size
    source_all = own_boxes * group_size
    interp_table = child_table(Q)
    offsets = proxy_offsets(Q, grid_cells)
    all_pivots = lax.all_gather(pivots, ("grp", "dev"), axis=0, tiled=True)
    slot_box = jnp.argsort(owner_slot)
    target_ids = jnp.arange(targets_all, dtype=jnp.int32)
    centre_x, centre_y = target_centres(target_ids, grid_cells)

    def one_box(local_id):
        child_box = lax.dynamic_index_in_dim(child_weights, local_id, 1, keepdims=False).reshape(
            2, 4 * proxies, targets_all // 4
        )
        return source_box(
            child_box,
            position * own_boxes + local_id,
            centre_x,
            centre_y,
            offsets,
            interp_table,
            grid_cells,
        )

    weights = lax.map(one_box, jnp.arange(own_boxes, dtype=jnp.int32))
    rank_ids = jnp.arange(RT, dtype=jnp.int32)
    outgoing = jnp.take(weights, slot_box, axis=3).reshape(
        own_boxes, 2, proxies, group_size, per_owner
    )
    incoming = route(outgoing, per_owner)
    my_boxes = lax.dynamic_slice_in_dim(slot_box, position * per_owner, per_owner)
    my_pivots = all_pivots[my_boxes]
    box_ids = jnp.arange(source_all, dtype=jnp.int32)

    def one_slot(slot_id):
        box_here = jnp.broadcast_to(my_boxes[slot_id], (RT,))
        point_x, point_y = pivot_points(box_here, my_pivots[slot_id], grid_cells)
        column = lax.dynamic_index_in_dim(incoming, slot_id, 3, keepdims=True)
        return skeleton_rows(point_x, point_y, box_ids, column, offsets, grid_cells)

    rows_all = lax.map(one_slot, jnp.arange(per_owner, dtype=jnp.int32))
    valid_rows = rank_ids[None, :] < ranks[my_boxes][:, None]
    masked = jnp.where(valid_rows[:, None, None, :], rows_all, 0.0)
    grouped = masked.reshape(per_owner, 2, source_all // 64, 2, grid_cells // 128, 2, RT).sum(
        axis=(3, 5)
    )
    grouped = grouped.reshape(per_owner, 2, source_all // 4, RT)
    result = jnp.transpose(grouped, (1, 3, 0, 2))
    return result


def solution(mesh):
    in_specs = (P(None, ("grp", "dev"), None, None, None), P(("grp", "dev"), None), P(), P())
    out_specs = P(None, None, ("grp", "dev"), None)
    return jax.shard_map(local, mesh=mesh, in_specs=in_specs, out_specs=out_specs, check_vma=False)
```

profile of v0, /device:TPU:0, one launch (start us, length us, event | category | flops | bytes accessed | tf_op | source)
XLA Modules:
  0.0 302.5 jit_solution(1841815222250460710)
XLA Ops:
  0.3 3.8 %sort.17 = (s32[256]{0:T(256)}, s32[256]{0:T(256)S(1)}) sort(s32[256]{0:T(256)} %param.11, s32[256]{0:T(256)S(1)} %iota.145), dimensions={0}, to_apply=%region_0.1 | sort | flops 2048 | bytes 4096 | tf_op jit(solution)/shard_map/jit(argsort)/sort | solution.py:178
  4.6 75.8 %while.33 = (s32[]{:T(128)}, f32[8,2,64,256]{3,2,1,0:T(8,128)S(1)}, s32[8]{0:T(128)S(1)}, f32[2,8,4,64,64]{4,3,2,1,0:T(8,128)}, s32[]{:T(128)}, /*index=5*/f32[2...) while((s32[]{:T(128)}, f32[8,2,64,256]{3,2,1,0:T(8,128)S(1)}, ...), condition=%wide.region_5.6_spmd.clone.clone.clone, body=%wide.region_4.5_spmd.clone.clone.clone.sunk | while | flops 102270112 | bytes 6063818 | solution.py:196
  10.8 1.5 multiply_add_fusion.7
  20.2 1.5 multiply_add_fusion.7
  58.1 1.5 multiply_add_fusion.7
  67.6 1.5 multiply_add_fusion.7
  81.2 2.2 gather_fusion.2
  83.4 2.6 copy_bitcast_fusion
  86.0 2.3 reshape.2055
  88.3 7.3 %all-to-all-start = ((f32[32,1,8192]{2,1,0:T(1,128)}), f32[32,1,8192]{2,1,0:T(1,128)S(1)}, u32[]{:S(2)}, u32[]{:S(2)}) async-start(f32[32,1,8192]{2,1,0:T(1,128)} %reshape.2055), calls=%async_computation | async-start | bytes 2097152 | tf_op jit(solution)/shard_map/all_to_all | solution.py:162
  95.6 56.0 %all_gather.3 = s32[256,32]{1,0:T(8,128)S(1)} all-gather(s32[8,32]{1,0:T(8,128)S(1)} %copy-done.1), channel_id=1, replica_groups=mesh['grp'=4,'dev'=8] {'grp','dev'}, dimensions={0}, use_global_device_ids=true | all-gather | bytes 33792 | tf_op jit(solution)/shard_map/all_gather | solution.py:177
  153.6 3.3 %reduce.2 = f32[32,8192]{1,0:T(8,128)S(1)} reduce(f32[32,1,8192]{2,1,0:T(1,128)S(1)} %all-to-all-done, f32[]{:T(128)} %broadcast.2997), dimensions={1}, to_apply=%all_to_all.11.reduce_sub_computation | reduce | bytes 2097156 | tf_op jit(solution)/shard_map/all_to_all | solution.py:162
  158.9 137.6 %while.34 = (s32[]{:T(128)}, f32[8,2,256,32]{2,3,1,0:T(8,128)}, s32[8]{0:T(128)S(1)}, s32[8]{0:T(128)S(1)}, s32[8,32]{1,0:T(8,128)S(1)}, /*index=5*/f32[256,2,64...) while((s32[]{:T(128)}, f32[8,2,256,32]{2,3,1,0:T(8,128)}, ...), condition=%wide.region_9.10_spmd.clone.clone.clone, body=%wide.region_6.9_spmd.clone.clone.clone.sunk | while | flops 9087867 | bytes 964994 | solution.py:212
  165.9 9.6 %subtract_reduce_fusion.2 = (f32[256,32]{0,1:T(8,128)S(1)}, f32[256,32]{0,1:T(8,128)S(1)}) fusion(f32[256,64]{0,1:T(8,128)S(1)} %get-tuple-element.1053, f32[256,64]{0,1:T(8,128)S(1)} %get-tuple-element.1054, f32[256,64]{0,1:T(8,128)S(1)} %broadcast_add_fusion.13, f32[32]{0:T(128)S(1)} %add_multiply_fusion.12, ...), kind=kLoop, calls=%fused_computation.87.clone.1 | loop fusion | flops 8896512 | bytes 377088 | tf_op jit(solution)/shard_map/while/body/eval_jaxpr/reduce_sum | solution.py:155
  183.1 9.6 %subtract_reduce_fusion.2 = (f32[256,32]{0,1:T(8,128)S(1)}, f32[256,32]{0,1:T(8,128)S(1)}) fusion(f32[256,64]{0,1:T(8,128)S(1)} %get-tuple-element.1053, f32[256,64]{0,1:T(8,128)S(1)} %get-tuple-element.1054, f32[256,64]{0,1:T(8,128)S(1)} %broadcast_add_fusion.13, f32[32]{0:T(128)S(1)} %add_multiply_fusion.12, ...), kind=kLoop, calls=%fused_computation.87.clone.1 | loop fusion | flops 8896512 | bytes 377088 | tf_op jit(solution)/shard_map/while/body/eval_jaxpr/reduce_sum | solution.py:155
  200.3 9.6 %subtract_reduce_fusion.2 = (f32[256,32]{0,1:T(8,128)S(1)}, f32[256,32]{0,1:T(8,128)S(1)}) fusion(f32[256,64]{0,1:T(8,128)S(1)} %get-tuple-element.1053, f32[256,64]{0,1:T(8,128)S(1)} %get-tuple-element.1054, f32[256,64]{0,1:T(8,128)S(1)} %broadcast_add_fusion.13, f32[32]{0:T(128)S(1)} %add_multiply_fusion.12, ...), kind=kLoop, calls=%fused_computation.87.clone.1 | loop fusion | flops 8896512 | bytes 377088 | tf_op jit(solution)/shard_map/while/body/eval_jaxpr/reduce_sum | solution.py:155
  217.5 9.6 %subtract_reduce_fusion.2 = (f32[256,32]{0,1:T(8,128)S(1)}, f32[256,32]{0,1:T(8,128)S(1)}) fusion(f32[256,64]{0,1:T(8,128)S(1)} %get-tuple-element.1053, f32[256,64]{0,1:T(8,128)S(1)} %get-tuple-element.1054, f32[256,64]{0,1:T(8,128)S(1)} %broadcast_add_fusion.13, f32[32]{0:T(128)S(1)} %add_multiply_fusion.12, ...), kind=kLoop, calls=%fused_computation.87.clone.1 | loop fusion | flops 8896512 | bytes 377088 | tf_op jit(solution)/shard_map/while/body/eval_jaxpr/reduce_sum | solution.py:155
  234.7 9.6 %subtract_reduce_fusion.2 = (f32[256,32]{0,1:T(8,128)S(1)}, f32[256,32]{0,1:T(8,128)S(1)}) fusion(f32[256,64]{0,1:T(8,128)S(1)} %get-tuple-element.1053, f32[256,64]{0,1:T(8,128)S(1)} %get-tuple-element.1054, f32[256,64]{0,1:T(8,128)S(1)} %broadcast_add_fusion.13, f32[32]{0:T(128)S(1)} %add_multiply_fusion.12, ...), kind=kLoop, calls=%fused_computation.87.clone.1 | loop fusion | flops 8896512 | bytes 377088 | tf_op jit(solution)/shard_map/while/body/eval_jaxpr/reduce_sum | solution.py:155
  251.8 9.6 %subtract_reduce_fusion.2 = (f32[256,32]{0,1:T(8,128)S(1)}, f32[256,32]{0,1:T(8,128)S(1)}) fusion(f32[256,64]{0,1:T(8,128)S(1)} %get-tuple-element.1053, f32[256,64]{0,1:T(8,128)S(1)} %get-tuple-element.1054, f32[256,64]{0,1:T(8,128)S(1)} %broadcast_add_fusion.13, f32[32]{0:T(128)S(1)} %add_multiply_fusion.12, ...), kind=kLoop, calls=%fused_computation.87.clone.1 | loop fusion | flops 8896512 | bytes 377088 | tf_op jit(solution)/shard_map/while/body/eval_jaxpr/reduce_sum | solution.py:155
  269.0 9.6 %subtract_reduce_fusion.2 = (f32[256,32]{0,1:T(8,128)S(1)}, f32[256,32]{0,1:T(8,128)S(1)}) fusion(f32[256,64]{0,1:T(8,128)S(1)} %get-tuple-element.1053, f32[256,64]{0,1:T(8,128)S(1)} %get-tuple-element.1054, f32[256,64]{0,1:T(8,128)S(1)} %broadcast_add_fusion.13, f32[32]{0:T(128)S(1)} %add_multiply_fusion.12, ...), kind=kLoop, calls=%fused_computation.87.clone.1 | loop fusion | flops 8896512 | bytes 377088 | tf_op jit(solution)/shard_map/while/body/eval_jaxpr/reduce_sum | solution.py:155
  286.2 9.6 %subtract_reduce_fusion.2 = (f32[256,32]{0,1:T(8,128)S(1)}, f32[256,32]{0,1:T(8,128)S(1)}) fusion(f32[256,64]{0,1:T(8,128)S(1)} %get-tuple-element.1053, f32[256,64]{0,1:T(8,128)S(1)} %get-tuple-element.1054, f32[256,64]{0,1:T(8,128)S(1)} %broadcast_add_fusion.13, f32[32]{0:T(128)S(1)} %add_multiply_fusion.12, ...), kind=kLoop, calls=%fused_computation.87.clone.1 | loop fusion | flops 8896512 | bytes 377088 | tf_op jit(solution)/shard_map/while/body/eval_jaxpr/reduce_sum | solution.py:155
  296.4 1.8 copy.77
  298.3 1.5 broadcast_select_fusion
  299.8 1.8 reduce_sum.37
  (424 shorter events, 74.5 us)
Async XLA Ops:
  0.0 152.2 %copy-start = (s32[256]{0:T(256)S(1)}, s32[256]{0:T(256)}, u32[]{:S(2)}) copy-start(s32[256]{0:T(256)} %param.10) | copy-start | bytes 3076
  86.0 9.6 %copy-start.1 = (s32[8,32]{1,0:T(8,128)S(1)}, s32[8,32]{1,0:T(8,128)}, u32[]{:S(2)}) copy-start(s32[8,32]{1,0:T(8,128)} %param.9) | copy-start | bytes 3076
  88.3 64.7 %all-to-all-start = ((f32[32,1,8192]{2,1,0:T(1,128)}), f32[32,1,8192]{2,1,0:T(1,128)S(1)}, u32[]{:S(2)}, u32[]{:S(2)}) async-start(f32[32,1,8192]{2,1,0:T(1,128)} %reshape.2055), calls=%async_computation | async-start | bytes 2097152 | tf_op jit(solution)/shard_map/all_to_all | solution.py:162
where the time goes:
time: 304 us; the launch traced here: 303 us
  other arithmetic  117 us (38%)
  loops' own time  62.9 us (21%)
  blocking collectives  56 us (18%)
  local copies, waits for them, and re-layouts  55.8 us (18%)
  starting transfers between devices  7.3 us (2%)
  matrix products  3.66 us (1%)
    reduce_sum x8, other arithmetic, skeleton_rows(): jnp.sum(cosine * weights[:, 0] - sine_part * weights[:, 1], axis=1)  76.5 us
    all_gather x1, blocking collectives, local(): all_pivots = lax.all_gather(pivots, ('grp', 'dev'), axis=0, tiled=True)  56 us
    another operation x1, loops' own time, local(): rows_all = lax.map(one_slot, jnp.arange(per_owner, dtype=jnp.int32))  39.3 us
    another operation x1, loops' own time, local(): weights = lax.map(one_box, jnp.arange(own_boxes, dtype=jnp.int32))  23.6 us
    add x8, other arithmetic, source_box(): spread[0] * cosine + spread[1] * sine_part  11.6 us
    dynamic_slice x16, local copies, waits for them, and re-layouts, local(): weights = lax.map(one_box, jnp.arange(own_boxes, dtype=jnp.int32))  10.6 us
    slice x16, local copies, waits for them, and re-layouts, source_box(): spread[1] * sine_part  9.04 us
    all_to_all x1, starting transfers between devices, route(): lax.all_to_all(outgoing, ('grp', 'dev'), split_axis=3, concat_axis=0, til...  7.3 us
  transfers between devices with their start and end apart: 1, of which 0 were waited for; matrix products, arithmetic and copies ran while one was open for 0% of the time, Pallas kernels for 0%

commit v1 on v0

v1 whole, which is shorter than its diff:
```python
import math

import jax
import jax.numpy as jnp
import numpy as np
from jax import lax
from jax.experimental import pallas as pl
from jax.experimental.pallas import tpu as pltpu
from jax.sharding import PartitionSpec as P

GRID = 2048
Q = 8
RT = 32
RMEAN = 10
SIDE = GRID // 32
WIDTH = GRID // 64
ROW = GRID // 64
COLS = GRID // 32
LANES = 128
R = Q * Q

SIN = (4.442867904603554, -7.30744348201647, 3.594788644821573, -0.7843755040132807)
COS = (1.414213496570567, -6.978850989042699, 5.73946118893746, -1.883563117820809, 0.31069847934250466)

F32 = jnp.float32
BF16 = jnp.bfloat16


def nodes():
    return np.cos(np.pi * (2.0 * np.arange(Q) + 1.0) / (2.0 * Q))


def lagrange(at, points):
    out = np.ones((Q, Q))
    for t in range(Q):
        for k in range(Q):
            if k != t:
                out[t] *= (points - at[k]) / (at[t] - at[k])
    return out


def child_table():
    c = nodes()
    halves = np.stack([lagrange(c, u - 0.5 + 0.5 * c) for u in (0.0, 1.0)])
    return np.einsum("uaj,vbk->abuvjk", halves, halves).reshape(R, 4 * R)


def split_table():
    table = child_table().astype(np.float32)
    high = table.astype(jnp.bfloat16)
    low = (table - high.astype(np.float32)).astype(jnp.bfloat16)
    return np.concatenate([high, low, high], axis=1)


def offsets():
    c = nodes()
    parent = SIDE / 2 - 0.5 + SIDE / 2 * c
    child = np.concatenate([SIDE * u / 2 + SIDE / 4 - 0.5 + SIDE / 4 * c for u in (0, 1)])
    return child, parent


def centre_rows(targets):
    a = np.arange(targets)
    x1 = (2 * WIDTH * (a // COLS) + WIDTH - 1) / (2 * GRID)
    x2 = (2 * WIDTH * (a % COLS) + WIDTH - 1) / (2 * GRID)
    c1 = (2 + np.sin(16 * np.pi * x1) * np.sin(16 * np.pi * x2)) / 16
    c2 = (2 + np.cos(16 * np.pi * x1) * np.cos(16 * np.pi * x2)) / 16
    child, parent = offsets()
    rows = [np.stack([c1, c2] + [np.zeros(targets)] * 6)]
    for o in (child, parent):
        for x in (x1, x2):
            turn = o[:, None] * x[None, :]
            rows.append(turn - np.floor(turn))
    return np.concatenate(rows).astype(np.float32)


def offset_columns():
    child, parent = offsets()
    return np.broadcast_to(np.concatenate([child, parent])[:, None], (3 * Q, LANES)).astype(np.float32)


def half_turn(phase):
    r = phase - jnp.round(phase)
    q = r * r
    s = SIN[3]
    for coefficient in SIN[2::-1]:
        s = s * q + coefficient
    s = s * r
    c = COS[4]
    for coefficient in COS[3::-1]:
        c = c * q + coefficient
    return s * s, s * c


def root(square):
    return jnp.sqrt(square)


def corner(own_boxes, box):
    position = lax.axis_index("grp") * lax.axis_size("dev") + lax.axis_index("dev")
    box_id = position * own_boxes + box
    return (box_id // ROW) * SIDE - GRID // 2, (box_id % ROW) * SIDE - GRID // 2


def outer(column, tile):
    return jnp.concatenate([column[j : j + 1] + tile for j in range(Q)], axis=0)


def source_kernel(own_boxes, targets, parents, weights_ref, table_ref, centre_ref, offset_ref, delta_ref):
    k1, k2 = corner(own_boxes, pl.program_id(0))
    k1f, k2f = k1.astype(F32), k2.astype(F32)
    offs = offset_ref[...]
    for g in range(targets // LANES):
        lanes = slice(g * LANES, (g + 1) * LANES)
        lane = lax.broadcasted_iota(jnp.int32, (1, LANES), 1)
        box = lane + g * LANES
        h1 = 2 * WIDTH * (box // COLS) + WIDTH - 1
        h2 = 2 * WIDTH * (box % COLS) + WIDTH - 1
        whole = ((h1 * k1 + h2 * k2) & (2 * GRID - 1)).astype(F32) * (1.0 / (2 * GRID))
        c1 = centre_ref[0:1, lanes]
        c2 = centre_ref[1:2, lanes]
        first = c1 * (k1f + offs)
        first = first * first
        second = c2 * (k2f + offs)
        second = second * second
        turn1 = centre_ref[8 : 8 + 2 * Q, lanes]
        turn2 = centre_ref[8 + 2 * Q : 8 + 4 * Q, lanes] + whole
        back1 = centre_ref[8 + 4 * Q : 8 + 5 * Q, lanes]
        back2 = centre_ref[8 + 5 * Q : 8 + 6 * Q, lanes] + whole
        parent_lane = (g * (COLS // 2)) % LANES + (lane % COLS) // 2
        pick = jnp.broadcast_to(parent_lane, (R, LANES))
        start = (g * (COLS // 2)) // LANES * LANES
        high, low = [], []
        for u in range(2):
            for v in range(2):
                one, two = slice(u * Q, (u + 1) * Q), slice(v * Q, (v + 1) * Q)
                phase = root(outer(first[one], second[two])) + outer(turn1[one], turn2[two])
                less, sine = half_turn(phase)
                spread = []
                for z in range(2):
                    w = weights_ref[z, 0, 2 * u + v, :, start : min(start + LANES, parents)]
                    if w.shape[1] < LANES:
                        w = jnp.concatenate([w] * (LANES // w.shape[1]), axis=1)
                    spread.append(jnp.take_along_axis(w, pick, axis=1, mode="promise_in_bounds"))
                wr, wi = spread
                both = jnp.concatenate(
                    [wr - (wr * less - wi * sine), wi - (wi * less + wr * sine)], axis=1
                )
                top = both.astype(BF16)
                high.append(top)
                low.append((both - top.astype(F32)).astype(BF16))
        moved = jnp.concatenate(high + high + low, axis=0)
        interp = jnp.dot(table_ref[...], moved, preferred_element_type=F32)
        ir, ii = interp[:, :LANES], interp[:, LANES:]
        parent = slice(2 * Q, 3 * Q)
        phase = root(outer(first[parent], second[parent])) + outer(back1, back2)
        less, sine = half_turn(phase)
        for z, part in enumerate((ir - (ir * less + ii * sine), ii - (ii * less - ir * sine))):
            top = part.astype(BF16)
            delta_ref[0, z, :, lanes] = top
            delta_ref[0, z, :, targets + g * LANES : targets + (g + 1) * LANES] = (
                part - top.astype(F32)
            ).astype(BF16)


def skeleton_kernel(
    own_boxes, targets, begin_ref, delta_ref, facts_ref, range_ref, place_ref, offset_ref, out_ref, picked, compact
):
    chunks = targets * RMEAN // LANES
    offs = offset_ref[2 * Q : 3 * Q]
    firsts = range_ref[0:1]
    ends = range_ref[1:2]
    corners = [corner(own_boxes, b) for b in range(own_boxes)]
    ranks_down = lax.broadcasted_iota(jnp.int32, (RT, LANES), 0)

    def one_chunk(c, carry):
        row = lax.broadcasted_iota(jnp.int32, (LANES, targets), 0) + c * LANES
        hot = jnp.where((firsts <= row) & (row < ends), 1.0, 0.0).astype(BF16)
        contract = (((1,), (1,)), ((), ()))
        facts = lax.dot_general(facts_ref[...], hot, contract, preferred_element_type=F32)
        picked[...] = lax.dot_general(
            delta_ref[...], jnp.concatenate([hot, hot], axis=1), contract, preferred_element_type=F32
        )
        facts = facts.astype(jnp.int32)
        here = lax.broadcasted_iota(jnp.int32, (1, LANES), 1) + c * LANES
        rank = here - (facts[2 * RT + 2 : 2 * RT + 3] * LANES + facts[2 * RT + 3 : 2 * RT + 4])
        mine = ranks_down == rank
        p1 = jnp.sum(jnp.where(mine, facts[:RT], 0), axis=0, keepdims=True)
        p2 = jnp.sum(jnp.where(mine, facts[RT : 2 * RT], 0), axis=0, keepdims=True)
        h1 = facts[2 * RT : 2 * RT + 1] * WIDTH + p1
        h2 = facts[2 * RT + 1 : 2 * RT + 2] * WIDTH + p2
        x1 = h1.astype(F32) * (1.0 / GRID)
        x2 = h2.astype(F32) * (1.0 / GRID)
        angle = jnp.concatenate([h1, h2], axis=0)
        angle = ((8 * angle) & (GRID - 1)).astype(F32) * (2.0 * math.pi / GRID)
        sines, cosines = jnp.sin(angle), jnp.cos(angle)
        c1 = (2.0 + sines[0:1] * sines[1:2]) * (1.0 / 16)
        c2 = (2.0 + cosines[0:1] * cosines[1:2]) * (1.0 / 16)
        turn1 = x1 * offs
        turn1 = turn1 - jnp.floor(turn1)
        turn2 = x2 * offs
        turn2 = turn2 - jnp.floor(turn2)
        first = c1 * (corners[0][0].astype(F32) + offs)
        first = first * first
        sums = []
        for b, (k1, k2) in enumerate(corners):
            whole = ((h1 * k1 + h2 * k2) & (GRID - 1)).astype(F32) * (1.0 / GRID)
            second = c2 * (k2.astype(F32) + offs)
            second = second * second
            phase = root(outer(first, second)) + outer(turn1, turn2 + whole)
            less, sine = half_turn(phase)
            wr = picked[2 * b * R : (2 * b + 1) * R]
            wi = picked[(2 * b + 1) * R : (2 * b + 2) * R]
            real = wr - (wr * less + wi * sine)
            imag = wi - (wi * less - wr * sine)
            sums.append((jnp.sum(real.reshape(Q, Q, LANES), axis=0), jnp.sum(imag.reshape(Q, Q, LANES), axis=0)))
        rows = [
            jnp.sum(sums[b][z] + sums[b + 1][z], axis=0, keepdims=True)
            for z in range(2)
            for b in range(0, own_boxes, 2)
        ]
        compact[c] = jnp.concatenate(rows, axis=0)
        return carry

    lax.fori_loop(0, chunks, one_chunk, 0)
    compact[chunks] = jnp.zeros_like(compact[0])
    boxes = LANES // RT

    def one_place(n, carry):
        chunk = begin_ref[n * boxes] // LANES
        place = jnp.broadcast_to(place_ref[pl.ds(n, 1)], (own_boxes, LANES))
        local = place - chunk * LANES
        within = local & (LANES - 1)
        near = jnp.take_along_axis(compact[chunk], within, axis=1, mode="promise_in_bounds")
        far = jnp.take_along_axis(compact[chunk + 1], within, axis=1, mode="promise_in_bounds")
        out_ref[n] = jnp.where(place < 0, 0.0, jnp.where(local >= LANES, far, near))
        return carry

    lax.fori_loop(0, targets // boxes, one_place, 0, unroll=4)


def local(child_weights, pivots, ranks, owner_slot):
    group_size = lax.axis_size("grp") * lax.axis_size("dev")
    own_boxes = child_weights.shape[1]
    parents = child_weights.shape[4]
    targets = ranks.shape[0]
    per_owner = targets // group_size
    vmem = pl.BlockSpec(memory_space=pltpu.VMEM)
    smem = pl.BlockSpec(memory_space=pltpu.SMEM)

    all_pivots = lax.all_gather(pivots, ("grp", "dev"), axis=0, tiled=True)
    offs = offset_columns()
    centre = centre_rows(targets)
    delta = pl.pallas_call(
        lambda *refs: source_kernel(own_boxes, targets, parents, *refs),
        grid=(own_boxes,),
        in_specs=[
            pl.BlockSpec((2, 1, 4, R, parents), lambda b: (0, b, 0, 0, 0)),
            pl.BlockSpec((R, 12 * R), lambda b: (0, 0)),
            pl.BlockSpec(centre.shape, lambda b: (0, 0)),
            pl.BlockSpec(offs.shape, lambda b: (0, 0)),
        ],
        out_specs=pl.BlockSpec((1, 2, R, 2 * targets), lambda b: (b, 0, 0, 0)),
        out_shape=jax.ShapeDtypeStruct((own_boxes, 2, R, 2 * targets), BF16),
        compiler_params=pltpu.CompilerParams(vmem_limit_bytes=48 << 20),
        cost_estimate=pl.CostEstimate(flops=200_000_000, bytes_accessed=4_000_000, transcendentals=0),
    )(child_weights, split_table(), centre, offs)

    ids = jnp.arange(targets, dtype=jnp.int32)
    starts = jnp.sum(jnp.where(owner_slot[:, None] < owner_slot[None, :], ranks[:, None], 0), axis=0)
    begin = jnp.sum(jnp.where(owner_slot[:, None] < ids[None, :], ranks[:, None], 0), axis=0)
    count = jnp.sum(jnp.where(owner_slot[:, None] == ids[None, :], ranks[:, None], 0), axis=0)
    ranges = jnp.stack([starts, starts + ranks])
    columns = all_pivots.T
    facts = jnp.concatenate(
        [columns // WIDTH, columns % WIDTH]
        + [row[None] for row in (ids // COLS, ids % COLS, starts // LANES, starts % LANES)]
        + [jnp.zeros((12, targets), jnp.int32)]
    ).astype(BF16)
    rank_ids = jnp.arange(RT, dtype=jnp.int32)
    place = jnp.where(rank_ids[None] < count[:, None], begin[:, None] + rank_ids[None], -1)
    place = place.reshape(-1, LANES)
    chunks = targets * RMEAN // LANES
    rows = pl.pallas_call(
        lambda *refs: skeleton_kernel(own_boxes, targets, *refs),
        in_specs=[smem, vmem, vmem, vmem, vmem, vmem],
        out_specs=vmem,
        out_shape=jax.ShapeDtypeStruct((place.shape[0], own_boxes, LANES), F32),
        scratch_shapes=[
            pltpu.VMEM((own_boxes * 2 * R, LANES), F32),
            pltpu.VMEM((chunks + 1, own_boxes, LANES), F32),
        ],
        compiler_params=pltpu.CompilerParams(vmem_limit_bytes=48 << 20),
    )(begin, delta.reshape(own_boxes * 2 * R, 2 * targets), facts, ranges, place, offs)

    received = lax.all_to_all(rows, ("grp", "dev"), split_axis=0, concat_axis=0, tiled=True)
    halves = own_boxes // 2
    pair = ROW // own_boxes
    received = received.reshape(group_size // (2 * pair), 2, pair, per_owner * RT // LANES, 2, halves, LANES // RT, RT)
    summed = received[:, 0] + received[:, 1]
    result = jnp.transpose(summed, (3, 6, 2, 5, 0, 1, 4))
    return result.reshape(2, RT, per_owner, group_size * own_boxes // 4)


def solution(mesh):
    in_specs = (P(None, ("grp", "dev"), None, None, None), P(("grp", "dev"), None), P(), P())
    out_specs = P(None, None, ("grp", "dev"), None)
    return jax.shard_map(local, mesh=mesh, in_specs=in_specs, out_specs=out_specs, check_vma=False)
```

time: 304 us -> 85.7 us (0.28)
  other arithmetic: 117 us -> 1.9 us
  loops' own time: 62.9 us -> 0 us
  local copies, waits for them, and re-layouts: 55.8 us -> 6.27 us
  Pallas kernels: 0 us -> 21 us
  starting transfers between devices: 7.3 us -> 0 us
  matrix products: 3.66 us -> 0 us
    reduce_sum x9 -> x1, other arithmetic: 78.4 us -> 0.91 us  [local(): jnp.sum(jnp.where(owner_slot[:, None] == ids[None, :], ranks[:, None], 0)...]
    another operation x2 -> x0, loops' own time: 62.9 us -> none  [the longest x1 39.3 us: local(): rows_all = lax.map(one_slot, jnp.arange(per_owner, dtype=jnp.int32))]
    pallas_call x0 -> x2, Pallas kernels: none -> 21 us  [the longest x1 15.1 us: local(): pl.pallas_call(lambda *refs: skeleton_kernel(own_boxes, targets, *refs),...]
    dynamic_slice x24 -> x0, local copies, waits for them, and re-layouts: 16 us -> none  [the longest x16 10.6 us: local(): weights = lax.map(one_box, jnp.arange(own_boxes, dtype=jnp.int32))]
    add x44 -> x2, other arithmetic: 13.1 us -> 0.89 us  [the longest x1 0.68 us: local(): ranges = jnp.stack([starts, starts + ranks])]
    all_to_all x0 -> x1, blocking collectives: none -> 12.1 us  [local(): lax.all_to_all(rows, ('grp', 'dev'), split_axis=0, concat_axis=0, tiled=T...]
    all_gather x1, blocking collectives: 56 us -> 44 us  [local(): all_pivots = lax.all_gather(pivots, ('grp', 'dev'), axis=0, tiled=True)]
    slice x24 -> x1, local copies, waits for them, and re-layouts: 10.2 us -> 0.1 us  [local(): summed = received[:, 0] + received[:, 1]]
  transfers between devices with their start and end apart: 1 -> 0, of which waited for: 0 -> 0; matrix products, arithmetic and copies ran while one was open for 0% -> 0% of each run, Pallas kernels for 0% -> 0%
where the time goes in v1:
time: 85.7 us; the launch traced here: 85.4 us
  blocking collectives  56.1 us (65%)
  Pallas kernels  21 us (25%)
  local copies, waits for them, and re-layouts  6.27 us (7%)
  other arithmetic  1.9 us (2%)
    all_gather x1, blocking collectives, local(): all_pivots = lax.all_gather(pivots, ('grp', 'dev'), axis=0, tiled=True)  44 us
    pallas_call x1, Pallas kernels, local(): pl.pallas_call(lambda *refs: skeleton_kernel(own_boxes, targets, *refs),...  15.1 us
    all_to_all x1, blocking collectives, local(): lax.all_to_all(rows, ('grp', 'dev'), split_axis=0, concat_axis=0, tiled=T...  12.1 us
    pallas_call x1, Pallas kernels, local(): pl.pallas_call(lambda *refs: source_kernel(own_boxes, targets, parents, *...  5.88 us
    unnamed x10, local copies, waits for them, and re-layouts  4.01 us

profile of v1, /device:TPU:0, one launch (start us, length us, event | category | flops | bytes accessed | tf_op | source)
XLA Modules:
  0.0 85.4 jit_solution(18198306518125496053)
XLA Ops:
  0.0 0.1 lt.79
  0.1 0.9 %select_reduce_fusion = (s32[256]{0:T(256)S(1)}, s32[256]{0:T(256)S(1)}, s32[256]{0:T(256)S(1)}) fusion(s32[256]{0:T(256)} %param.9, s32[256]{0:T(256)} %param.10), kind=kLoop, calls=%fused_computation.1 | loop fusion | flops 589056 | bytes 5120 | tf_op jit(solution)/shard_map/reduce_sum | solution.py:272
  1.0 0.7 add.75
  1.7 0.1 lt.82
  1.9 0.1 copy.27
  1.9 0.1 add.76
  2.0 0.1 copy.29
  2.1 0.1 copy.30
  2.2 0.1 copy.28
  2.3 44.0 %all_gather.3 = s32[256,32]{1,0:T(8,128)S(1)} all-gather(s32[8,32]{1,0:T(8,128)} %param.8), channel_id=1, replica_groups=mesh['grp'=4,'dev'=8] {'grp','dev'}, dimensions={0}, use_global_device_ids=true | all-gather | bytes 33792 | tf_op jit(solution)/shard_map/all_gather | solution.py:251
  46.3 0.1 copy.26
  46.4 0.0 copy-start
  46.4 1.6 %copy-done = f32[2,8,4,64,64]{4,3,2,1,0:T(8,128)S(1)} copy-done((f32[2,8,4,64,64]{4,3,2,1,0:T(8,128)S(1)}, f32[2,8,4,64,64]{4,3,2,1,0:T(8,128)}, u32[]{:S(2)}) %copy-start) | copy-done | bytes 1048600
  48.0 0.9 %copy-done.1 = bf16[64,768]{1,0:T(8,128)(2,1)S(1)} copy-done((bf16[64,768]{1,0:T(8,128)(2,1)S(1)}, bf16[64,768]{1,0:T(8,128)(2,1)}, u32[]{:S(2)}) %copy-start.1) | copy-done | bytes 98328
  48.9 0.8 copy-done.2
  49.7 0.7 copy-done.3
  50.4 5.9 %shard_map.73 = bf16[8,2,64,512]{3,2,1,0:T(8,128)(2,1)S(1)} custom-call(f32[2,8,4,64,64]{4,3,2,1,0:T(8,128)S(1)} %copy-done, bf16[64,768]{1,0:T(8,128)(2,1)S(1)} %copy-done.1, f32[56,256]{1,0:T(8,128)S(1)} %copy-done.2, f32[24,128]{1,0:T(8,128)S(1)} %copy-done.3), custom_call_target="tpu_custom_call" | custom-call | flops 200000000 | bytes 4000000 | tf_op jit(solution)/shard_map/pallas_call | solution.py:254
  56.3 0.2 concatenate.4.refs_2_
  56.5 15.1 %shard_map.74 = f32[64,8,128]{2,1,0:T(8,128)S(1)} custom-call(s32[256]{0:T(256)S(1)} %get-tuple-element.7.refs_0_, bf16[1024,512]{1,0:T(8,128)(2,1)S(1)} %bitcast.36, bf16[80,256]{1,0:T(8,128)(2,1)S(1)} %concatenate.4.refs_2_, s32[2,256]{1,0:T(2,128)S(1)} %pad_add_fusion.refs_3_, s32[64,128]{1,0:T(8,128)S(1)} %add_select_fusion.2.refs_4_, ...), custom_call_target="tpu_custom_call" | custom-call | tf_op jit(solution)/shard_map/pallas_call | solution.py:284
  71.6 12.1 %all_to_all.5 = f32[64,8,128]{2,1,0:T(8,128)S(1)} all-to-all(f32[64,8,128]{2,1,0:T(8,128)S(1)} %shard_map.74), channel_id=1, replica_groups=mesh['grp'=4,'dev'=8] {'grp','dev'}, dimensions={0} | all-to-all | bytes 524288 | tf_op jit(solution)/shard_map/all_to_all | solution.py:296
  83.7 0.4 reshape.147
  84.1 0.1 fusion.9
  84.2 0.2 copy_add_fusion
  84.5 0.9 %copy.33 = f32[2,32,8,64]{3,2,1,0:T(8,128)} copy(f32[2,32,8,64]{1,3,2,0:T(8,128)S(1)} %bitcast.37) | data formatting | bytes 262144 | tf_op jit(solution)/shard_map/reshape | solution.py:302
  (15 shorter events, 0.1 us)
Async XLA Ops:
  2.1 54.4 %copy-start.4 = (f32[24,128]{1,0:T(8,128)S(1)}, f32[24,128]{1,0:T(8,128)}, u32[]{:S(2)}) copy-start(f32[24,128]{1,0:T(8,128)} %constant.89.clone.refs_3_.refs_5_) | copy-start | bytes 36868
  46.4 1.6 %copy-start = (f32[2,8,4,64,64]{4,3,2,1,0:T(8,128)S(1)}, f32[2,8,4,64,64]{4,3,2,1,0:T(8,128)}, u32[]{:S(2)}) copy-start(f32[2,8,4,64,64]{4,3,2,1,0:T(8,128)} %refs_0_.1) | copy-start | bytes 3145732
  48.0 0.9 %copy-start.1 = (bf16[64,768]{1,0:T(8,128)(2,1)S(1)}, bf16[64,768]{1,0:T(8,128)(2,1)}, u32[]{:S(2)}) copy-start(bf16[64,768]{1,0:T(8,128)(2,1)} %constant.87.clone.refs_1_) | copy-start | bytes 294916
  48.9 0.8 copy-start.2
  49.7 0.7 copy-start.3
